TPU v7x, 128 devices: a whole 4x4x4 slice. The times are simulated.
128 devices in a mesh: dp: 64 (over x_lo, z, y, core), tensor: 2 (over x_hi).
Axes of the slice: x: 4 (x_hi: 2, x_lo: 2; x = x_hi * 2 + x_lo), y: 4, z: 4, core: 2. Of those that a mesh axis runs over, the one named last changes fastest.
Arguments:
- tokens: bfloat16 [65536, 1024], P('dp'), may hold values from -6 to 6
- norm_gain: float32 [1024], replicated, may hold values from 0.5 to 1.5
- norm_shift: float32 [1024], replicated, may hold values from -4 to 4
- qkv_weight: bfloat16 [1024, 3, 1024], P(None, None, 'tensor'), may hold values from -0.25 to 0.25
- merge_weight: bfloat16 [1024, 1024], P('tensor'), may hold values from -0.5 to 0.5
- up_weight: bfloat16 [1024, 4096], P(None, 'tensor'), may hold values from -0.1875 to 0.1875
- inner_shift: float32 [4096], P('tensor'), may hold values from -6 to 6
- down_weight: bfloat16 [4096, 1024], P('tensor'), may hold values from -0.09375 to 0.09375
- outer_shift: float32 [1024], replicated, may hold values from -6 to 6
- cotangent: bfloat16 [65536, 1024], P('dp'), may hold values from -6 to 6
Outputs:
- block_out: bfloat16 [65536, 1024], P('dp')
- token_grad: bfloat16 [65536, 1024], P('dp')
- gain_grad: float32 [1024], replicated
- shift_grad: float32 [1024], replicated
- qkv_grad: float32 [1024, 3, 1024], P(None, None, 'tensor')
- merge_grad: float32 [1024, 1024], P('tensor')
- up_grad: float32 [1024, 4096], P(None, 'tensor')
- inner_grad: float32 [4096], P('tensor')
- down_grad: float32 [4096, 1024], P('tensor')
- outer_grad: float32 [1024], replicated
All inputs are finite; a program needn't handle non-finite values.
Results may differ from a plain program's by a relative error of at most 0.0065.
The roundings to bfloat16 on the way count: a program that leaves them out, or rounds other values in their place, can miss the bound.
Values sent between devices are 32-bit elements; how exact they have to be, the bound alone decides.
No kernel may reach another device: no remote copies, remote signals or barrier semaphores. Data moves between devices by JAX's collectives and lax.ppermute only.
A program may use at most 256 MiB of HBM per device.

v0:
```python
import jax
import jax.numpy as jnp
from jax import lax
from jax.sharding import PartitionSpec as P

HEAD = 64
ROT = 32


epsilon = 1e-05


def angle_tables(length):
    half = ROT // 2
    positions = jnp.arange(length, dtype=jnp.float32)
    rates = 10000.0 ** (-jnp.arange(half, dtype=jnp.float32) / half)
    angles = positions[:, None] * rates[None, :]
    return (jnp.cos(angles)[:, None, :], jnp.sin(angles)[:, None, :])


def turn_pairs(block, cosine, sine):
    half = ROT // 2
    paired = block[..., :ROT].reshape(block.shape[:-1] + (half, 2))
    leading = paired[..., 0]
    trailing = paired[..., 1]
    turned = jnp.stack(
        [leading * cosine - trailing * sine, trailing * cosine + leading * sine], axis=-1
    )
    turned = turned.reshape(block.shape[:-1] + (ROT,))
    return jnp.concatenate([turned, block[..., ROT:]], axis=-1)


def rotate(block, cosine, sine):
    return turn_pairs(block, cosine, sine)


def unrotate(block, cosine, sine):
    return turn_pairs(block, cosine, -sine)


def masked_scores(query, keys, causal):
    scores = jnp.einsum("qhd,khd->hqk", query, keys, preferred_element_type=jnp.float32) * HEAD ** (
        -0.5
    )
    return jnp.where(causal, scores, -1e30)


def body(
    tokens,
    norm_gain,
    norm_shift,
    qkv_weight,
    merge_weight,
    up_weight,
    inner_shift,
    down_weight,
    outer_shift,
    cotangent,
):
    length, width = tokens.shape
    local = merge_weight.shape[0]
    heads = local // HEAD
    inputs = tokens.astype(jnp.float32)
    average = jnp.mean(inputs, axis=-1, keepdims=True)
    centred = inputs - average
    inverse = lax.rsqrt(jnp.mean(centred * centred, axis=-1, keepdims=True) + epsilon)
    unit = centred * inverse
    normed = (unit * norm_gain + norm_shift).astype(jnp.bfloat16)
    qkv_flat = qkv_weight.reshape(width, 3 * local)
    joined = jnp.dot(normed, qkv_flat, preferred_element_type=jnp.float32).reshape(
        length, 3, heads, HEAD
    )
    cosine, sine = angle_tables(length)
    query = rotate(joined[:, 0], cosine, sine).astype(jnp.bfloat16)
    keys = rotate(joined[:, 1], cosine, sine).astype(jnp.bfloat16)
    values = joined[:, 2].astype(jnp.bfloat16)
    causal = jnp.arange(length)[None, :] <= jnp.arange(length)[:, None]
    scores = masked_scores(query, keys, causal)
    peak = jnp.max(scores, axis=-1, keepdims=True)
    expo = jnp.exp(scores - peak)
    summed = jnp.sum(expo, axis=-1, keepdims=True)
    probs = expo / summed
    logsum = peak + jnp.log(summed)
    mixed = jnp.einsum(
        "hqk,khd->qhd", probs.astype(jnp.bfloat16), values, preferred_element_type=jnp.float32
    )
    heads_out = mixed.astype(jnp.bfloat16).reshape(length, local)
    attention = jnp.dot(heads_out, merge_weight, preferred_element_type=jnp.float32)
    before = jnp.dot(normed, up_weight, preferred_element_type=jnp.float32) + inner_shift
    active = jax.nn.gelu(before, approximate=True).astype(jnp.bfloat16)
    partial_value = attention + jnp.dot(active, down_weight, preferred_element_type=jnp.float32)
    branches = lax.psum(partial_value, "tensor")
    block_out = (inputs + branches + outer_shift).astype(jnp.bfloat16)
    upstream = cotangent.astype(jnp.float32)
    outer_g = jnp.sum(upstream, axis=0)
    down_g = jnp.einsum("tf,td->fd", active, cotangent, preferred_element_type=jnp.float32)
    d_active = jnp.einsum("td,fd->tf", cotangent, down_weight, preferred_element_type=jnp.float32)
    gelu_pull = jax.vjp(lambda inside: jax.nn.gelu(inside, approximate=True), before)[1]
    d_before = gelu_pull(d_active)[0].astype(jnp.bfloat16)
    inner_g = jnp.sum(d_before.astype(jnp.float32), axis=0)
    up_g = jnp.einsum("tm,tf->mf", normed, d_before, preferred_element_type=jnp.float32)
    d_normed_ffn = jnp.einsum("tf,mf->tm", d_before, up_weight, preferred_element_type=jnp.float32)
    merge_g = jnp.einsum("tl,td->ld", heads_out, cotangent, preferred_element_type=jnp.float32)
    d_heads = jnp.einsum("td,ld->tl", cotangent, merge_weight, preferred_element_type=jnp.float32)
    d_heads = d_heads.astype(jnp.bfloat16).reshape(length, heads, HEAD)
    again = jnp.exp(masked_scores(query, keys, causal) - logsum)
    d_probs = jnp.einsum("qhd,khd->hqk", d_heads, values, preferred_element_type=jnp.float32)
    d_values = jnp.einsum(
        "hqk,qhd->khd", again.astype(jnp.bfloat16), d_heads, preferred_element_type=jnp.float32
    )
    inner = jnp.sum(again * d_probs, axis=-1, keepdims=True)
    d_scores = (again * (d_probs - inner)).astype(jnp.bfloat16)
    d_query = jnp.einsum(
        "hqk,khd->qhd", d_scores, keys, preferred_element_type=jnp.float32
    ) * HEAD ** (-0.5)
    d_keys = jnp.einsum(
        "hqk,qhd->khd", d_scores, query, preferred_element_type=jnp.float32
    ) * HEAD ** (-0.5)
    d_joined = jnp.stack(
        [unrotate(d_query, cosine, sine), unrotate(d_keys, cosine, sine), d_values], axis=1
    )
    d_joined = d_joined.astype(jnp.bfloat16).reshape(length, 3 * local)
    qkv_g = jnp.einsum("tm,tc->mc", normed, d_joined, preferred_element_type=jnp.float32).reshape(
        width, 3, local
    )
    d_normed = d_normed_ffn + jnp.einsum(
        "tc,mc->tm", d_joined, qkv_flat, preferred_element_type=jnp.float32
    )
    d_normed = lax.psum(d_normed, "tensor")
    gain_g = jnp.sum(d_normed * unit, axis=0)
    shift_g = jnp.sum(d_normed, axis=0)
    d_unit = d_normed * norm_gain
    centre_term = jnp.mean(d_unit, axis=-1, keepdims=True)
    slope_term = jnp.mean(d_unit * unit, axis=-1, keepdims=True)
    token_grad = (upstream + inverse * (d_unit - centre_term - unit * slope_term)).astype(
        jnp.bfloat16
    )
    gain_g, shift_g, qkv_g, merge_g, up_g, inner_g, down_g, outer_g = lax.psum(
        (gain_g, shift_g, qkv_g, merge_g, up_g, inner_g, down_g, outer_g), "dp"
    )
    return (block_out, token_grad, gain_g, shift_g, qkv_g, merge_g, up_g, inner_g, down_g, outer_g)


def solution(mesh):
    return jax.shard_map(
        body,
        mesh=mesh,
        in_specs=(
            P("dp", None),
            P(),
            P(),
            P(None, None, "tensor"),
            P("tensor", None),
            P(None, "tensor"),
            P("tensor"),
            P("tensor", None),
            P(),
            P("dp", None),
        ),
        out_specs=(
            P("dp", None),
            P("dp", None),
            P(),
            P(),
            P(None, None, "tensor"),
            P("tensor", None),
            P(None, "tensor"),
            P("tensor"),
            P("tensor", None),
            P(),
        ),
        check_vma=False,
    )
```

profile of v0, /device:TPU:1, one launch (start us, length us, event | category | flops | bytes accessed | tf_op | source)
XLA Modules:
  0.0 1115.6 jit_solution(427891351476050903)
XLA Ops:
  11.7 4.7 copy.25
  16.4 5.6 fusion.29
  35.8 4.5 subtract_convert_fusion.1
  40.2 3.2 pad_maximum_fusion.8
  47.5 15.3 %fusion.54 = (f32[8,1024]{1,0:T(8,128)S(1)}, f32[8,1024,1024]{1,2,0:T(8,128)}) fusion(bf16[1024,8,32]{0,2,1:T(8,128)(2,1)} %slice.123, bf16[1024,8,32]{0,2,1:T(8,128)(2,1)} %reshape.166, bf16[1024,8,32]{0,2,1:T(8,128)(2,1)} %slice.124, bf16[1024,8,32]{0,2,1:T(8,128)(2,1)} %reshape.164, pred[1024,1024]{0,1:T(8,128)(4,1)} %iota_compare_fusion), kind=kOutput, calls=%fused_computation.95 | convolution fusion | flops 1103093760 | bytes 36732928 | tf_op jit(solution)/shard_map/qhd,khd->hqk/dot_general | solution.py:42
  62.8 13.2 %fusion = f32[8,1024]{1,0:T(8,128)S(1)} fusion(f32[8,1024,1024]{1,2,0:T(8,128)} %get-tuple-element.48, f32[8,1024]{1,0:T(8,128)S(1)} %get-tuple-element.47), kind=kLoop, calls=%fused_computation.6 | loop fusion | flops 16769024 | bytes 33619968 | tf_op jit(solution)/shard_map/reduce_sum | solution.py:81
  77.4 23.0 %multiply_reduce_fusion = (f32[8,1024]{1,0:T(8,128)S(1)}, f32[8,1024,1024]{1,2,0:T(8,128)}) fusion(f32[8,1024,1024]{1,2,0:T(8,128)} %get-tuple-element.48, f32[8,1024]{1,0:T(8,128)S(1)} %log_add_fusion, bf16[1024,8,64]{0,2,1:T(8,128)(2,1)S(1)} %bitcast.86, f32[1024,3,8,64]{0,3,2,1:T(8,128)} %copy-done.4), kind=kOutput, calls=%fused_computation.1 | convolution fusion | flops 1098899456 | bytes 69271552 | tf_op jit(solution)/shard_map/qhd,khd->hqk/dot_general | solution.py:107
  100.4 28.5 %multiply_convert_fusion = bf16[8,1024,1024]{1,2,0:T(8,128)(2,1)} fusion(f32[8,1024,1024]{1,2,0:T(8,128)} %get-tuple-element.50, f32[8,1024,1024]{1,2,0:T(8,128)} %get-tuple-element.48, f32[8,1024]{1,0:T(8,128)S(1)} %get-tuple-element.49, f32[8,1024]{1,0:T(8,128)S(1)} %log_add_fusion), kind=kLoop, calls=%fused_computation | loop fusion | flops 33554432 | bytes 83951616 | tf_op jit(solution)/shard_map/convert_element_type | solution.py:112
  128.9 10.5 multiply_bitcast_fusion.1
  139.4 12.6 %multiply_bitcast_fusion = f32[1024,8,64]{0,2,1:T(8,128)} fusion(bf16[8,1024,1024]{1,2,0:T(8,128)(2,1)} %multiply_convert_fusion, bf16[1024,8,32]{0,2,1:T(8,128)(2,1)} %slice.124, bf16[1024,8,32]{0,2,1:T(8,128)(2,1)} %reshape.164), kind=kOutput, calls=%fused_computation.56 | convolution fusion | flops 1076363264 | bytes 19922944 | tf_op jit(solution)/shard_map/hqk,qhd->khd/dot_general | solution.py:116
  160.8 14.5 %fusion.33 = bf16[1024,1,8,64]{0,3,2,1:T(8,128)(2,1)} fusion(bf16[1024,8,64]{0,2,1:T(8,128)(2,1)} %bitcast.87, f32[8,1024,1024]{1,2,0:T(8,128)} %get-tuple-element.48, f32[8,1024]{1,0:T(8,128)S(1)} %log_add_fusion), kind=kOutput, calls=%fused_computation.59 | convolution fusion | flops 1090519040 | bytes 35684352 | tf_op jit(solution)/shard_map/hqk,qhd->khd/dot_general | solution.py:108
  175.4 15.1 %fusion.36 = bf16[8,64,1024]{2,1,0:T(8,128)(2,1)} fusion(f32[8,1024,1024]{1,2,0:T(8,128)} %get-tuple-element.48, f32[8,1024]{1,0:T(8,128)S(1)} %fusion, f32[8,1024]{1,0:T(8,128)S(1)} %get-tuple-element.47, f32[1024,3,8,64]{0,3,2,1:T(8,128)} %copy-done.4), kind=kOutput, calls=%fused_computation.61 | convolution fusion | flops 1099431936 | bytes 35717120 | tf_op jit(solution)/shard_map/hqk,khd->qhd/dot_general | solution.py:84
  196.1 5.1 multiply_subtract_fusion.1
  205.2 3.2 pad_maximum_fusion.3
  210.4 9.5 fusion.50
  220.0 12.5 %convert_reduce_fusion = (f32[2048]{0:T(1024)S(1)}, bf16[1024,2048]{1,0:T(8,128)(2,1)S(1)}, bf16[1024,2048]{1,0:T(8,128)(2,1)S(1)}) fusion(f32[1024,2048]{1,0:T(8,128)} %fusion.50, f32[2048]{0:T(1024)S(1)} %copy-done.24, bf16[1024,1024]{1,0:T(8,128)(2,1)S(1)} %copy-done.12, bf16[2048,1024]{1,0:T(8,128)(2,1)S(1)} %copy-done.23), kind=kOutput, calls=%fused_computation.20 | convolution fusion | flops 4347394048 | bytes 23085056 | tf_op jit(solution)/shard_map/td,fd->tf/dot_general | solution.py:97
  232.5 4.5 fusion.56
  237.1 4.5 fusion.55
  242.9 3.4 convolution_add_fusion
  249.3 5.1 convolution_add_fusion.1
  254.5 4.6 fusion.57
  259.1 6.5 fusion.31
  265.7 6.9 fusion.58
  272.6 7.1 fusion.47
  279.8 184.3 %all-reduce.8.cloned.1.call-done = (f32[1024,1024]{1,0:T(8,128)}, f32[1024,1024]{1,0:T(8,128)}) async-done(((f32[1024,1024]{1,0:T(8,128)}, f32[1024,1024]{1,0:T(8,128)}), (f32[1024,1024]{1,0:T(8,128)}, f32[1024,1024]{1,0:T(8,128)})) %all-reduce.8.cloned.1.call-update) | async-done | bytes 8388624 | tf_op jit(solution)/shard_map/psum | solution.py:92
  464.1 3.9 fusion.24
  468.2 5.2 convert_reduce_fusion.2
  473.4 273.8 %all-reduce = (f32[1024]{0:T(1024)}, f32[1024]{0:T(1024)}, f32[2048]{0:T(1024)}, f32[1024]{0:T(1024)}) all-reduce(f32[1024]{0:T(1024)S(1)} %get-tuple-element.10, f32[1024]{0:T(1024)S(1)} %get-tuple-element.13, f32[2048]{0:T(1024)S(1)} %get-tuple-element.24, f32[1024]{0:T(1024)S(1)} %get-tuple-element.29), channel_id=1, replica_groups=mesh['dp'=64,'tensor'=2] {'dp'}, use_global_device_ids=true, to_apply=%region_10.11 | all-reduce | flops 5120 | bytes 40960 | tf_op jit(solution)/shard_map/psum | solution.py:138
  747.2 343.3 %all-reduce.6.cloned.1.call-done = (f32[1024,3,512]{2,0,1:T(8,128)}, f32[512,1024]{1,0:T(8,128)}, f32[1024,2048]{1,0:T(8,128)}, f32[2048,1024]{1,0:T(8,128)}) async-done(((f32[1024,3,512]{2,0,1:T(8,128)}, f32[512,1024]{1,0:T(8,128)}, f32[1024,2048]{1,0:T(8,128)}, f32[2048,1024]{1,0:T(8,128)}), (f32[1024,3,512]{2,0,1:T(8,128)}, f32[512,1024]{1,0:T(8,128)}, f32[1024,2048]{1,0:T(8,128)}, ...) | async-done | bytes 25165840 | tf_op jit(solution)/shard_map/psum | solution.py:138
  1090.5 6.9 copy.44
  1099.1 4.3 copy.46
  1104.9 3.4 copy.47
  (102 shorter events, 52.0 us)
Async XLA Ops:
  7.2 68.9 %copy-start = (bf16[512,1024]{1,0:T(8,128)(2,1)S(1)}, bf16[512,1024]{1,0:T(8,128)(2,1)}, u32[]{:S(2)}) copy-start(bf16[512,1024]{1,0:T(8,128)(2,1)} %param.14) | copy-start | bytes 3145732
  7.2 456.9 %all-reduce.8.cloned.1.call-start = ((), (), s32[]{:S(2)}) async-start(), calls=%async_computation.1 | async-start | bytes 16777216 | tf_op jit(solution)/shard_map/psum | solution.py:92
  9.3 7.2 copy-start.1
  9.3 7.2 copy-start.20
  9.3 7.1 copy-start.25
  22.0 2.7 copy-start.4
  62.8 13.3 %copy-start.11 = (bf16[1024,1024]{1,0:T(8,128)(2,1)S(1)}, bf16[1024,1024]{1,0:T(8,128)(2,1)}, u32[]{:S(2)}) copy-start(bf16[1024,1024]{1,0:T(8,128)(2,1)} %param.19) | copy-start | bytes 6291460
  77.4 23.0 %copy-start.5 = (bf16[1024,512]{0,1:T(8,128)(2,1)}, bf16[1024,512]{0,1:T(8,128)(2,1)S(1)}, u32[]{:S(2)}) copy-start(bf16[1024,512]{0,1:T(8,128)(2,1)S(1)} %convolution_convert_fusion) | copy-start | bytes 3145732
  210.4 9.5 copy-start.12
  210.4 9.5 copy-start.23
  210.4 9.5 copy-start.24
  220.0 12.6 %copy-start.22 = (bf16[1024,2048]{1,0:T(8,128)(2,1)S(1)}, bf16[1024,2048]{1,0:T(8,128)(2,1)}, u32[]{:S(2)}) copy-start(bf16[1024,2048]{1,0:T(8,128)(2,1)} %param.15) | copy-start | bytes 12582916
  232.5 4.6 copy-start.26
  232.5 4.6 copy-start.28
  237.1 4.5 copy-start.16
  237.1 4.5 copy-start.18
  237.1 4.6 copy-start.17
  237.1 4.6 copy-start.19
  242.9 3.4 copy-start.6
  246.3 3.0 copy-start.8
  254.5 836.1 %all-reduce.6.cloned.1.call-start = ((), (), s32[]{:S(2)}) async-start(), calls=%async_computation | async-start | bytes 50331648 | tf_op jit(solution)/shard_map/psum | solution.py:138
  254.5 4.6 copy-start.10
  259.1 6.5 copy-start.13
  259.1 6.5 copy-start.29
  265.7 6.9 copy-start.27
  279.8 188.2 %copy-start.21 = (f32[1024]{0:T(1024)S(1)}, f32[1024]{0:T(1024)}, u32[]{:S(2)}) copy-start(f32[1024]{0:T(1024)} %param.18) | copy-start | bytes 12292
  464.1 3.9 copy-start.2
  464.1 4.1 copy-start.14
  1090.5 6.9 copy-start.15
  1090.5 8.6 copy-start.3
  1097.4 5.9 slice-start
  1099.1 5.8 slice-start.1
  (2 other events, 2.9 us)
Sparse Core Ops, SparseCore 0:
  254.6 209.4 all-reduce.7
  468.0 622.4 all-reduce.5
where the time goes:
time: 1120 us
  waiting for transfers between devices  528 us (47%)
  blocking collectives  274 us (24%)
  matrix products  163 us (15%)
  other arithmetic  75.2 us (7%)
  local copies, waits for them, and re-layouts  61.3 us (5%)
  between operations  14.9 us (1%)
    psum x1, waiting for transfers between devices, body(): lax.psum((gain_g, shift_g, qkv_g, merge_g, up_g, inner_g, down_g, outer_g...  343 us
    psum x1, blocking collectives, body(): lax.psum((gain_g, shift_g, qkv_g, merge_g, up_g, inner_g, down_g, outer_g...  274 us
    psum x1, waiting for transfers between devices, body(): branches = lax.psum(partial_value, 'tensor')  184 us
    unnamed x69, local copies, waits for them, and re-layouts  28.6 us
    convert_element_type x1, other arithmetic, body(): d_scores = (again * (d_probs - inner)).astype(jnp.bfloat16)  28.5 us
    dot_general x1, matrix products, body(): jnp.einsum('qhd,khd->hqk', d_heads, values, preferred_element_type=jnp.fl...  23 us
  transfers between devices with their start and end apart: 2, of which 2 were waited for; matrix products, arithmetic and copies ran while one was open for 3% of the time, Pallas kernels for 0%

commit v1 on v0

v1 whole, which is shorter than its diff:
```python
import functools

import jax
import jax.numpy as jnp
import numpy as np
from jax import lax
from jax.experimental import pallas as pl
from jax.experimental.pallas import tpu as pltpu
from jax.sharding import Mesh
from jax.sharding import PartitionSpec as P

F32 = jnp.float32
BF16 = jnp.bfloat16
HEAD = 64
ROT = 32
PAIR = 2 * HEAD
epsilon = 1e-05


def nn(a, b):
    return jnp.dot(a, b, preferred_element_type=F32)


def nt(a, b):
    return lax.dot_general(a, b, (((1,), (1,)), ((), ())), preferred_element_type=F32)


def tn(a, b):
    return lax.dot_general(a, b, (((0,), (0,)), ((), ())), preferred_element_type=F32)


def rotary_tables(length):
    half = ROT // 2
    rates = 10000.0 ** (-jnp.arange(half, dtype=F32) / half)
    angles = jnp.arange(length, dtype=F32)[:, None] * rates[None, :]
    cosine = jnp.repeat(jnp.cos(angles), 2, axis=1)
    sine = jnp.repeat(jnp.sin(angles), 2, axis=1)
    sine = sine * jnp.where(jnp.arange(ROT) % 2 == 0, -1.0, 1.0)
    cosine = jnp.concatenate([cosine, jnp.ones((length, HEAD - ROT), F32)], axis=1)
    sine = jnp.concatenate([sine, jnp.zeros((length, HEAD - ROT), F32)], axis=1)
    return jnp.tile(cosine, (1, 2)), jnp.tile(sine, (1, 2))


def swap_pairs(x):
    lane = lax.broadcasted_iota(jnp.int32, x.shape, 1)
    return jnp.where(lane % 2 == 0, pltpu.roll(x, PAIR - 1, 1), pltpu.roll(x, 1, 1))


def project_kernel(tok, gain, shift, w, mw, cot, cos, sin, normed, normed_t, q, k, v, dh):
    x = tok[...].astype(F32)
    centred = x - jnp.mean(x, axis=1, keepdims=True)
    inverse = lax.rsqrt(jnp.mean(centred * centred, axis=1, keepdims=True) + epsilon)
    n = (centred * inverse * gain[...] + shift[...]).astype(BF16)
    normed[...] = n
    normed_t[...] = n.T
    dh[...] = nt(cot[...], mw[...]).astype(BF16)
    c = cos[...]
    s = sin[...]
    for which, ref in enumerate((q, k, v)):
        joined = nn(n, w[which])
        if which == 2:
            ref[...] = joined.astype(BF16)
            continue
        for p in range(joined.shape[1] // PAIR):
            block = joined[:, p * PAIR : (p + 1) * PAIR]
            turned = (block * c + swap_pairs(block) * s).astype(BF16)
            if which == 0:
                turned = turned * jnp.asarray(HEAD**-0.5, BF16)
            ref[:, p * PAIR : (p + 1) * PAIR] = turned


def project(tok, gain, shift, w3, mw, cot, cos, sin, rows=256):
    length, width = tok.shape
    local = mw.shape[0]

    def row_block(n):
        return pl.BlockSpec((rows, n), lambda i: (i, 0))

    def full(*s):
        return pl.BlockSpec(s, lambda i: (0,) * len(s))

    def out(*s):
        return jax.ShapeDtypeStruct(s, BF16)

    return pl.pallas_call(
        project_kernel,
        grid=(length // rows,),
        in_specs=[
            row_block(width),
            full(1, width),
            full(1, width),
            full(3, width, local),
            full(local, width),
            row_block(width),
            row_block(PAIR),
            row_block(PAIR),
        ],
        out_specs=[row_block(width), pl.BlockSpec((width, rows), lambda i: (0, i))]
        + [row_block(local)] * 4,
        out_shape=[out(length, width), out(width, length)] + [out(length, local)] * 4,
        compiler_params=pltpu.CompilerParams(vmem_limit_bytes=48 << 20),
        cost_estimate=pl.CostEstimate(
            flops=8 * length * width * local, bytes_accessed=16 << 20, transcendentals=0
        ),
        name="project",
    )(tok, gain, shift, w3, mw, cot, cos, sin)


def attend_kernel(q, k, v, do, cos, sin, ho, dq, dk, dv, dk_sum, dv_sum, *, block):
    length = q.shape[0]
    lane = lax.broadcasted_iota(jnp.int32, (block, PAIR), 1)
    causal = lax.broadcasted_iota(jnp.int32, (block, block), 1) <= lax.broadcasted_iota(
        jnp.int32, (block, block), 0
    )
    dk_sum[...] = jnp.zeros_like(dk_sum)
    dv_sum[...] = jnp.zeros_like(dv_sum)
    zero = jnp.zeros((block, PAIR), BF16)
    for i in range(length // block):
        rows = slice(i * block, (i + 1) * block)
        seen = (i + 1) * block
        q_rows = q[rows, :]
        do_rows = do[rows, :]
        keys = k[0:seen, :]
        values = v[0:seen, :]
        mixed = d_query = None
        for h in range(2):
            mine = (lane < HEAD) if h == 0 else (lane >= HEAD)
            q_head = jnp.where(mine, q_rows, zero)
            do_head = jnp.where(mine, do_rows, zero)
            scores = nt(q_head, keys)
            edge = jnp.where(causal, scores[:, seen - block :], -1e30)
            if i > 0:
                edge = jnp.concatenate([scores[:, : seen - block], edge], axis=1)
            scores = edge
            expo = jnp.exp(scores - jnp.max(scores, axis=1, keepdims=True))
            probs = expo * (1.0 / jnp.sum(expo, axis=1, keepdims=True))
            probs_low = probs.astype(BF16)
            mixed_head = nn(probs_low, values)
            d_probs = nt(do_head, values)
            inner = jnp.sum(probs * d_probs, axis=1, keepdims=True)
            d_scores = (probs * (d_probs - inner)).astype(BF16)
            d_query_head = nn(d_scores, keys)
            dv_sum[0:seen, :] += tn(probs_low, do_head)
            dk_sum[0:seen, :] += tn(d_scores, q_head)
            mixed = mixed_head if h == 0 else jnp.where(mine, mixed_head, mixed)
            d_query = d_query_head if h == 0 else jnp.where(mine, d_query_head, d_query)
        ho[rows, :] = mixed.astype(BF16)
        d_query = d_query * HEAD**-0.5
        dq[rows, :] = (d_query * cos[rows, :] - swap_pairs(d_query) * sin[rows, :]).astype(BF16)
    for i in range(length // block):
        rows = slice(i * block, (i + 1) * block)
        d_keys = dk_sum[rows, :]
        dk[rows, :] = (d_keys * cos[rows, :] - swap_pairs(d_keys) * sin[rows, :]).astype(BF16)
        dv[rows, :] = dv_sum[rows, :].astype(BF16)


def attend(q, k, v, do, cos, sin, block=512):
    length, local = q.shape
    pairs = local // PAIR
    spec = pl.BlockSpec((length, PAIR), lambda p: (0, p))
    table = pl.BlockSpec((length, PAIR), lambda p: (0, 0))
    out = jax.ShapeDtypeStruct((length, local), BF16)
    return pl.pallas_call(
        functools.partial(attend_kernel, block=block),
        grid=(pairs,),
        in_specs=[spec] * 4 + [table] * 2,
        out_specs=[spec] * 4,
        out_shape=[out] * 4,
        scratch_shapes=[pltpu.VMEM((length, PAIR), F32)] * 2,
        compiler_params=pltpu.CompilerParams(vmem_limit_bytes=48 << 20),
        cost_estimate=pl.CostEstimate(
            flops=20 * length * length * PAIR * pairs,
            bytes_accessed=8 << 20,
            transcendentals=length * length * pairs,
        ),
        name="attend",
    )(q, k, v, do, cos, sin)


gelu_rate = float(np.sqrt(2 / np.pi))


def feed_kernel(normed, normed_t, cot, up, shift, down, out, dn, dg, ug, ig):
    j = pl.program_id(0)
    n = normed[...]
    c = cot[...]
    v = nn(n, up[...]) + shift[...]
    da = nt(c, down[...])
    square = v * v
    t = jnp.tanh(gelu_rate * v * (1.0 + 0.044715 * square))
    h = 0.5 * (1.0 + t)
    active = (v * h).astype(BF16)
    slope = h + (0.5 * gelu_rate) * v * (1.0 - t * t) * (1.0 + (3 * 0.044715) * square)
    d_pre = (da * slope).astype(BF16)
    ig[...] = jnp.sum(d_pre.astype(F32), axis=0, keepdims=True)
    o = nn(active, down[...])
    d = nt(d_pre, up[...])

    @pl.when(j == 0)
    def _():
        out[...] = o
        dn[...] = d

    @pl.when(j > 0)
    def _():
        out[...] += o
        dn[...] += d

    grad = tn(active, c)
    for y in range(4):
        for core in range(2):
            rows = grad.shape[0] // 8
            first = (2 * y + core) * rows
            for z in range(4):
                spot = spot_of(z, y, core, 0)

                @pl.when(j == z)
                def _():
                    dg[core * 16 + spot] = grad[first : first + rows, :]

    grad = nn(normed_t[...], d_pre)
    for z in range(4):
        for y in range(4):
            for core in range(2):
                rows = grad.shape[0] // 32
                first = ((z * 4 + y) * 2 + core) * rows
                ug[core * 16 + spot_of(z, y, core, 1)] = grad[first : first + rows, :]


def feed(normed, normed_t, cot, up, shift, down):
    length, width = normed.shape
    hidden = up.shape[1]
    step = hidden // 4

    def full(*s):
        return pl.BlockSpec(s, lambda i: (0,) * len(s))

    return pl.pallas_call(
        feed_kernel,
        grid=(4,),
        in_specs=[
            full(length, width),
            full(width, length),
            full(length, width),
            pl.BlockSpec((width, step), lambda i: (0, i)),
            pl.BlockSpec((1, step), lambda i: (0, i)),
            pl.BlockSpec((step, width), lambda i: (i, 0)),
        ],
        out_specs=[
            full(length, width),
            full(length, width),
            full(32, hidden // 32, width),
            pl.BlockSpec((32, width // 32, step), lambda i: (0, 0, i)),
            pl.BlockSpec((1, step), lambda i: (0, i)),
        ],
        out_shape=[
            jax.ShapeDtypeStruct(s, F32)
            for s in (
                (length, width),
                (length, width),
                (32, hidden // 32, width),
                (32, width // 32, hidden),
                (1, hidden),
            )
        ],
        compiler_params=pltpu.CompilerParams(vmem_limit_bytes=60 << 20),
        cost_estimate=pl.CostEstimate(
            flops=12 * length * width * hidden,
            bytes_accessed=36 << 20,
            transcendentals=length * hidden,
        ),
        name="feed",
    )(normed, normed_t, cot, up, shift, down)


def tail_kernel(normed_t, ho, cot, dq, dk, dv, grads):
    which = pl.program_id(0)
    n = normed_t[...]
    for w, ref in enumerate((dq, dk, dv)):

        @pl.when(which == w)
        def _():
            grads[0] = nn(n, ref[...])

    @pl.when(which == 3)
    def _():
        g = tn(ho[...], cot[...])
        half = g.shape[1] // 2
        grads[0, :half, :] = g[:, :half]
        grads[0, half:, :] = g[:, half:]


def tail_grads(normed_t, ho, cot, dq, dk, dv):
    width, length = normed_t.shape
    local = ho.shape[1]
    assert 2 * local == width

    def full(*s):
        return pl.BlockSpec(s, lambda i: (0,) * len(s))

    return pl.pallas_call(
        tail_kernel,
        grid=(4,),
        in_specs=[full(width, length), full(length, local), full(length, width)]
        + [full(length, local)] * 3,
        out_specs=pl.BlockSpec((1, width, local), lambda i: (i, 0, 0)),
        out_shape=jax.ShapeDtypeStruct((4, width, local), F32),
        compiler_params=pltpu.CompilerParams(vmem_limit_bytes=48 << 20),
        cost_estimate=pl.CostEstimate(
            flops=8 * length * width * local, bytes_accessed=16 << 20, transcendentals=0
        ),
        name="tail",
    )(normed_t, ho, cot, dq, dk, dv)


AXES = ("xlo", "z", "y", "core", "tensor")
RINGS = ("z", "y", "core")
DIRECTIONS = (("y", 0), ("z", 0), ("y", 1), ("z", 1))
SWAP = ((0, 1), (1, 0))


def partner(place, bit):
    return place ^ 1 if bit == 0 else 3 - place


def bit_at(place, bit):
    return int(place in (1, 2)) if bit == 0 else int(place >= 2)


def order_of(core, part):
    return [(core + 2 * part + step) % 4 for step in range(4)]


def spot_of(z, y, core, part):
    spot = 0
    for direction in order_of(core, part):
        axis, bit = DIRECTIONS[direction]
        spot = 2 * spot + bit_at(y if axis == "y" else z, bit)
    return spot


def step_pairs(part, step):
    pairs = []
    for z in range(4):
        for y in range(4):
            for core in range(2):
                axis, bit = DIRECTIONS[order_of(core, part)[step]]
                z2, y2 = (z, partner(y, bit)) if axis == "y" else (partner(z, bit), y)
                pairs.append(((z * 4 + y) * 2 + core, (z2 * 4 + y2) * 2 + core))
    return pairs


def step_bit(part, step):
    table = np.zeros((32,), np.int32)
    for z in range(4):
        for y in range(4):
            for core in range(2):
                axis, bit = DIRECTIONS[order_of(core, part)[step]]
                table[(z * 4 + y) * 2 + core] = bit_at(y if axis == "y" else z, bit)
    return jnp.asarray(table)[lax.axis_index(RINGS)]


def halves(x, bit):
    h = x.shape[0] // 2
    keep = lax.dynamic_slice_in_dim(x, bit * h, h, 0)
    send = lax.dynamic_slice_in_dim(x, (1 - bit) * h, h, 0)
    return keep, send


def scatter_rings(x, part):
    for step in range(4):
        keep, send = halves(x, step_bit(part, step))
        x = keep + lax.ppermute(send, RINGS, step_pairs(part, step))
    return x


def gather_rings(x, part):
    for step in reversed(range(4)):
        other = lax.ppermute(x, RINGS, step_pairs(part, step))
        first = step_bit(part, step) == 0
        x = jnp.where(
            first, jnp.concatenate([x, other], axis=0), jnp.concatenate([other, x], axis=0)
        )
    return x


def exchange(x, axis):
    return lax.ppermute(x, axis, SWAP)


def sum_small(v):
    for step in range(4):
        v = v + lax.ppermute(v, RINGS, step_pairs(0, step))
    v = v + exchange(v, "core")
    return v + exchange(v, "xlo")


def body(
    tokens,
    norm_gain,
    norm_shift,
    qkv_weight,
    merge_weight,
    up_weight,
    inner_shift,
    down_weight,
    outer_shift,
    cotangent,
):
    length, width = tokens.shape
    local = merge_weight.shape[0]
    hidden = up_weight.shape[1]
    core = lax.axis_index("core")
    cos, sin = rotary_tables(length)
    w3 = qkv_weight.transpose(1, 0, 2)
    gain, shift = norm_gain[None], norm_shift[None]
    normed, normed_t, q, k, v, dh = project(
        tokens, gain, shift, w3, merge_weight, cotangent, cos, sin
    )
    out_ffn, dn_ffn, down_g, up_g, inner_g = feed(
        normed, normed_t, cotangent, up_weight, inner_shift[None], down_weight
    )

    down_keep, down_send = halves(down_g, core)
    up_keep, up_send = halves(up_g, core)
    down_x = down_keep + exchange(down_send, "core")
    up_x = up_keep + exchange(up_send, "core")
    down_x = scatter_rings(down_x, 0)
    up_x = scatter_rings(up_x, 1)
    down_x = (down_x + exchange(down_x, "xlo")).reshape(hidden // 32, width)
    up_x = (up_x + exchange(up_x, "xlo")).reshape(width // 32, hidden)
    down_out = lax.all_gather(down_x, RINGS, tiled=True)
    up_out = lax.all_gather(up_x, RINGS, tiled=True)

    ho, dq, dk, dv = attend(q, k, v, dh, cos, sin)

    inputs = tokens.astype(F32)
    average = jnp.mean(inputs, axis=-1, keepdims=True)
    centred = inputs - average
    inverse = lax.rsqrt(jnp.mean(centred * centred, axis=-1, keepdims=True) + epsilon)
    unit = centred * inverse
    upstream = cotangent.astype(F32)

    chunks = 2
    rows = length // chunks
    slices = [slice(i * rows, (i + 1) * rows) for i in range(chunks)]
    outs = []
    for r in slices:
        mine = nn(ho[r], merge_weight) + out_ffn[r]
        outs.append((inputs[r] + (mine + exchange(mine, "tensor")) + outer_shift).astype(BF16))
    block_out = jnp.concatenate(outs, axis=0)

    grads = []
    gain_g = jnp.zeros((width,), F32)
    shift_g = jnp.zeros((width,), F32)
    for r in slices:
        mine = dn_ffn[r] + nt(dq[r], w3[0]) + nt(dk[r], w3[1]) + nt(dv[r], w3[2])
        gain_g = gain_g + jnp.sum(mine * unit[r], axis=0)
        shift_g = shift_g + jnp.sum(mine, axis=0)
        d_normed = mine + exchange(mine, "tensor")
        d_unit = d_normed * norm_gain
        centre = jnp.mean(d_unit, axis=-1, keepdims=True)
        slope = jnp.mean(d_unit * unit[r], axis=-1, keepdims=True)
        grads.append((upstream[r] + inverse[r] * (d_unit - centre - unit[r] * slope)).astype(BF16))
    token_grad = jnp.concatenate(grads, axis=0)

    late = tail_grads(normed_t, ho, cotangent, dq, dk, dv)
    late_keep, late_send = halves(late, core)
    late_x = late_keep + exchange(late_send, "core")
    parts = [scatter_rings(late_x[i], i) for i in range(2)]
    parts = [x + exchange(x, "xlo") for x in parts]
    parts = [gather_rings(x, i) for i, x in enumerate(parts)]
    own = jnp.stack(parts)
    other = exchange(own, "core")
    first = core == 0
    qkv_out = jnp.stack(
        [
            jnp.where(first, own[0], other[0]),
            jnp.where(first, own[1], other[1]),
            jnp.where(first, other[0], own[0]),
        ],
        axis=1,
    )
    merge_out = jnp.where(first, other[1], own[1])
    merge_out = jnp.concatenate([merge_out[:local], merge_out[local:]], axis=1)

    small = jnp.concatenate(
        [
            gain_g[None],
            shift_g[None],
            jnp.sum(upstream, axis=0)[None],
            inner_g.reshape(hidden // width, width),
            jnp.zeros((8 - 3 - hidden // width, width), F32),
        ],
        axis=0,
    )
    small = sum_small(small)
    pair = small[:2] + exchange(small[:2], "tensor")
    return (
        block_out,
        token_grad,
        pair[0],
        pair[1],
        qkv_out,
        merge_out,
        up_out,
        small[3 : 3 + hidden // width].reshape(hidden),
        down_out,
        small[2],
    )


def solution(mesh):
    dp = AXES[:4]
    finer = Mesh(mesh.devices.reshape(2, 4, 4, 2, 2), AXES)
    return jax.shard_map(
        body,
        mesh=finer,
        in_specs=(
            P(dp, None),
            P(),
            P(),
            P(None, None, "tensor"),
            P("tensor", None),
            P(None, "tensor"),
            P("tensor"),
            P("tensor", None),
            P(),
            P(dp, None),
        ),
        out_specs=(
            P(dp, None),
            P(dp, None),
            P(),
            P(),
            P(None, None, "tensor"),
            P("tensor", None),
            P(None, "tensor"),
            P("tensor"),
            P("tensor", None),
            P(),
        ),
        check_vma=False,
    )
```

time: 1120 us -> 584 us (0.52)
  waiting for transfers between devices: 528 us -> 215 us
  blocking collectives: 274 us -> 0 us
  matrix products: 163 us -> 13.2 us
  Pallas kernels: 0 us -> 89.5 us
  starting transfers between devices: 0.08 us -> 86.5 us
  between operations: 14.9 us -> 35.8 us
    psum x2 -> x0, waiting for transfers between devices: 528 us -> none  [the longest x1 343 us: body(): lax.psum((gain_g, shift_g, qkv_g, merge_g, up_g, inner_g, down_g, outer_g...]
    psum x1 -> x0, blocking collectives: 274 us -> none  [body(): lax.psum((gain_g, shift_g, qkv_g, merge_g, up_g, inner_g, down_g, outer_g...]
    ppermute x0 -> x43, waiting for transfers between devices: none -> 215 us  [the longest x15 100 us: exchange(): return lax.ppermute(x, axis, SWAP)]
    dot_general x18 -> x8, matrix products: 163 us -> 13.2 us  [the longest x6 7.21 us: nt(): lax.dot_general(a, b, (((1,), (1,)), ((), ())), preferred_element_type=F32)]
    pallas_call x0 -> x4, Pallas kernels: none -> 89.5 us  [the longest x1 42.8 us: feed(): pl.pallas_call(feed_kernel, grid=(4,), in_specs=[full(length, width), ful...]
    ppermute x0 -> x43, starting transfers between devices: none -> 86.4 us  [the longest x15 43.6 us: exchange(): return lax.ppermute(x, axis, SWAP)]
    add x1 -> x31, other arithmetic: 0.01 us -> 31.1 us  [the longest x16 16.4 us: scatter_rings(): x = keep + lax.ppermute(send, RINGS, step_pairs(part, step))]
    dynamic_slice x0 -> x23, local copies, waits for them, and re-layouts: none -> 25.5 us  [the longest x19 23.1 us: halves(): send = lax.dynamic_slice_in_dim(x, (1 - bit) * h, h, 0)]
  transfers between devices with their start and end apart: 2 -> 45, of which waited for: 2 -> 31; matrix products, arithmetic and copies ran while one was open for 3% -> 19% of each run, Pallas kernels for 0% -> 7%
where the time goes in v1:
time: 584 us; the launch traced here: 574 us
  waiting for transfers between devices  215 us (37%)
  Pallas kernels  89.5 us (15%)
  starting transfers between devices  86.5 us (15%)
  other arithmetic  79.1 us (14%)
  local copies, waits for them, and re-layouts  54.5 us (9%)
  between operations  35.8 us (6%)
  matrix products  13.2 us (2%)
    ppermute x15, waiting for transfers between devices, exchange(): return lax.ppermute(x, axis, SWAP)  100 us
    ppermute x16, waiting for transfers between devices, scatter_rings(): x = keep + lax.ppermute(send, RINGS, step_pairs(part, step))  92.4 us
    ppermute x15, starting transfers between devices, exchange(): return lax.ppermute(x, axis, SWAP)  43.6 us
    pallas_call x1, Pallas kernels, feed(): pl.pallas_call(feed_kernel, grid=(4,), in_specs=[full(length, width), ful...  42.8 us
    ppermute x16, starting transfers between devices, scatter_rings(): x = keep + lax.ppermute(send, RINGS, step_pairs(part, step))  32.4 us
    pallas_call x1, Pallas kernels, attend(): pl.pallas_call(functools.partial(attend_kernel, block=block), grid=(pairs...  27.8 us
    unnamed x87, local copies, waits for them, and re-layouts  24.4 us
    dynamic_slice x19, local copies, waits for them, and re-layouts, halves(): send = lax.dynamic_slice_in_dim(x, (1 - bit) * h, h, 0)  23.1 us
  transfers between devices with their start and end apart: 45, of which 31 were waited for; matrix products, arithmetic and copies ran while one was open for 19% of the time, Pallas kernels for 7%

profile of v1, /device:TPU:1, one launch (start us, length us, event | category | flops | bytes accessed | tf_op | source)
XLA Modules:
  0.0 573.7 jit_solution(9907656561679379518)
XLA Ops:
  8.6 9.3 %project.1 = (bf16[1024,1024]{1,0:T(8,128)(2,1)}, bf16[1024,1024]{1,0:T(8,128)(2,1)}, bf16[1024,512]{1,0:T(8,128)(2,1)S(1)}, bf16[1024,512]{1,0:T(8,128)(2,1)S(1...) custom-call(bf16[1024,1024]{1,0:T(8,128)(2,1)} %tok.1, f32[1,1024]{1,0:T(1,128)S(1)} %bitcast.97, ...), custom_call_target="tpu_custom_call" | custom-call | flops 4294967296 | bytes 16777216 | tf_op jit(solution)/shard_map/project/pallas_call | solution.py:85
  20.8 42.8 %feed.1 = (f32[1024,1024]{1,0:T(8,128)}, f32[1024,1024]{1,0:T(8,128)}, f32[32,64,1024]{2,1,0:T(8,128)}, f32[32,32,2048]{2,1,0:T(8,128)}, f32[1,2048]{1,0:T(1,128)}) custom-call(bf16[1024,1024]{1,0:T(8,128)(2,1)} %get-tuple-element.30.normed, bf16[1024,1024]{1,0:T(8,128)(2,1)} %get-tuple-element.31.normed_t, bf16[1024,1024]{1,0:T(8,128)(2,1)} %cot.5, ...), custom_call_target="tpu_custom_call" | custom-call | flops 25769803776 | bytes 37748736 | tf_op jit(solution)/shard_map/feed/pallas_call | solution.py:238
  63.6 4.7 constant_dynamic-slice_fusion.9
  71.0 5.9 %collective-permute-done.31 = f32[16,32,2048]{2,1,0:T(8,128)} collective-permute-done((f32[16,32,2048]{2,1,0:T(8,128)}, f32[16,32,2048]{2,1,0:T(8,128)}, u32[]{:S(2)}, u32[]{:S(2)}) %collective-permute-start.31) | collective-permute-done | bytes 4194336 | tf_op jit(solution)/shard_map/ppermute | solution.py:388
  76.9 4.2 dynamic-slice_add_fusion.1
  89.1 21.6 %collective-permute-done.32 = f32[8,32,2048]{2,1,0:T(8,128)} collective-permute-done((f32[8,32,2048]{2,1,0:T(8,128)S(1)}, f32[8,32,2048]{2,1,0:T(8,128)}, u32[]{:S(2)}, u32[]{:S(2)}) %collective-permute-start.32) | collective-permute-done | bytes 2097184 | tf_op jit(solution)/shard_map/ppermute | solution.py:373
  116.7 10.7 %collective-permute-done.33 = f32[4,32,2048]{2,1,0:T(8,128)} collective-permute-done((f32[4,32,2048]{2,1,0:T(8,128)S(1)}, f32[4,32,2048]{2,1,0:T(8,128)}, u32[]{:S(2)}, u32[]{:S(2)}) %collective-permute-start.33) | collective-permute-done | bytes 1048608 | tf_op jit(solution)/shard_map/ppermute | solution.py:373
  131.3 5.9 %collective-permute-done.34 = f32[2,32,2048]{2,1,0:T(8,128)S(1)} collective-permute-done((f32[2,32,2048]{2,1,0:T(8,128)S(1)}, f32[2,32,2048]{2,1,0:T(8,128)S(1)}, u32[]{:S(2)}, u32[]{:S(2)}) %collective-permute-start.34) | collective-permute-done | bytes 524320 | tf_op jit(solution)/shard_map/ppermute | solution.py:373
  150.1 4.8 constant_dynamic-slice_fusion.4
  154.9 5.1 collective-permute-start.37
  160.1 7.1 %collective-permute-done.37 = f32[16,64,1024]{2,1,0:T(8,128)} collective-permute-done((f32[16,64,1024]{2,1,0:T(8,128)}, f32[16,64,1024]{2,1,0:T(8,128)}, u32[]{:S(2)}, u32[]{:S(2)}) %collective-permute-start.37) | collective-permute-done | bytes 4194336 | tf_op jit(solution)/shard_map/ppermute | solution.py:388
  167.2 4.4 dynamic-slice_add_fusion
  176.4 27.8 %attend.1 = (bf16[1024,512]{1,0:T(8,128)(2,1)S(1)}, bf16[1024,512]{1,0:T(8,128)(2,1)S(1)}, bf16[1024,512]{1,0:T(8,128)(2,1)S(1)}, bf16[1024,512]{1,0:T(8,128)(2,1)S(1)}) custom-call(bf16[1024,512]{1,0:T(8,128)(2,1)} %copy-done.9, bf16[1024,512]{1,0:T(8,128)(2,1)} %copy-done.10, bf16[1024,512]{1,0:T(8,128)(2,1)} %copy-done.11, bf16[1024,512]{1,0:T(8,128)(2,1)} %copy-done.12, ...), custom_call_target="tpu_custom_call" | custom-call | flops 10737418240 | bytes 8388608 | tf_op jit(solution)/shard_map/attend/pallas_call | solution.py:163
  204.2 9.7 %tail.1 = f32[4,1024,512]{2,1,0:T(8,128)} custom-call(bf16[1024,1024]{1,0:T(8,128)(2,1)} %get-tuple-element.31.normed_t, bf16[1024,512]{1,0:T(8,128)(2,1)S(1)} %get-tuple-element.29.ho, bf16[1024,1024]{1,0:T(8,128)(2,1)} %cot.5, bf16[1024,512]{1,0:T(8,128)(2,1)S(1)} %get-tuple-element.34.dq, bf16[1024,512]{1,0:T(8,128)(2,1)S(1)} %get-tuple-element.35.dk, ...), custom_call_target="tpu_custom_call" | custom-call | flops 4294967296 | bytes 16777216 | tf_op jit(solution)/shard_map/tail/pallas_call | solution.py:301
  213.9 4.6 constant_dynamic-slice_fusion.16
  228.5 12.3 %collective-permute-done.39 = f32[4,64,1024]{2,1,0:T(8,128)} collective-permute-done((f32[4,64,1024]{2,1,0:T(8,128)}, f32[4,64,1024]{2,1,0:T(8,128)}, u32[]{:S(2)}, u32[]{:S(2)}) %collective-permute-start.39) | collective-permute-done | bytes 1048608 | tf_op jit(solution)/shard_map/ppermute | solution.py:373
  249.2 5.2 collective-permute-done.40
  256.5 9.4 %collective-permute-start.41 = (f32[1,64,1024]{2,1,0:T(8,128)S(1)}, f32[1,64,1024]{2,1,0:T(8,128)}, u32[]{:S(2)}, u32[]{:S(2)}) collective-permute-start(f32[1,64,1024]{2,1,0:T(8,128)S(1)} %constant_dynamic-slice_fusion), channel_id=1, source_target_pairs={{0,48},{2,6},{4,52},{6,2},{8,56},{10,14},{12,60},{14,10},{16,32},{... | collective-permute-start | bytes 786440 | tf_op jit(solution)/shard_map/ppermute | solution.py:373
  278.1 4.5 dynamic-slice_add_fusion.2
  293.0 12.6 %collective-permute-done.21 = f32[512,512]{1,0:T(8,128)} collective-permute-done((f32[512,512]{1,0:T(8,128)}, f32[512,512]{1,0:T(8,128)}, u32[]{:S(2)}, u32[]{:S(2)}) %collective-permute-start.21) | collective-permute-done | bytes 1048608 | tf_op jit(solution)/shard_map/ppermute | solution.py:373
  324.8 7.3 %collective-permute-done.13 = f32[256,512]{1,0:T(8,128)} collective-permute-done((f32[256,512]{1,0:T(8,128)}, f32[256,512]{1,0:T(8,128)}, u32[]{:S(2)}, u32[]{:S(2)}) %collective-permute-start.13) | collective-permute-done | bytes 524320 | tf_op jit(solution)/shard_map/ppermute | solution.py:373
  349.9 12.5 %collective-permute-done.25 = f32[64,512]{1,0:T(8,128)S(1)} collective-permute-done((f32[64,512]{1,0:T(8,128)S(1)}, f32[64,512]{1,0:T(8,128)S(1)}, u32[]{:S(2)}, u32[]{:S(2)}) %collective-permute-start.25) | collective-permute-done | bytes 131104 | tf_op jit(solution)/shard_map/ppermute | solution.py:388
  382.1 6.9 %collective-permute-done.28 = f32[256,512]{1,0:T(8,128)S(1)} collective-permute-done((f32[256,512]{1,0:T(8,128)S(1)}, f32[256,512]{1,0:T(8,128)S(1)}, u32[]{:S(2)}, u32[]{:S(2)}) %collective-permute-start.28) | collective-permute-done | bytes 524320 | tf_op jit(solution)/shard_map/ppermute | solution.py:379
  400.9 7.1 %collective-permute-done.29 = f32[512,512]{1,0:T(8,128)} collective-permute-done((f32[512,512]{1,0:T(8,128)}, f32[512,512]{1,0:T(8,128)}, u32[]{:S(2)}, u32[]{:S(2)}) %collective-permute-start.29) | collective-permute-done | bytes 1048608 | tf_op jit(solution)/shard_map/ppermute | solution.py:379
  417.5 9.4 %collective-permute-start.30 = (f32[2,1024,512]{2,1,0:T(8,128)}, f32[2,1024,512]{2,1,0:T(8,128)}, u32[]{:S(2)}, u32[]{:S(2)}) collective-permute-start(f32[2,1024,512]{2,1,0:T(8,128)} %pad_maximum_fusion.1), channel_id=1, source_target_pairs={{0,2},{2,0},{1,3},{3,1},{4,6},{6,4},{5,7},{7,5},{8,10},{10,8},{9,1... | collective-permute-start | bytes 12582920 | tf_op jit(solution)/shard_map/ppermute | solution.py:388
  428.5 32.2 %collective-permute-done.3 = f32[512,1024]{1,0:T(8,128)} collective-permute-done((f32[512,1024]{1,0:T(8,128)}, f32[512,1024]{1,0:T(8,128)}, u32[]{:S(2)}, u32[]{:S(2)}) %collective-permute-start.3) | collective-permute-done | bytes 2097184 | tf_op jit(solution)/shard_map/ppermute | solution.py:388
  460.8 5.4 multiply_reduce_fusion.1
  474.1 31.6 %collective-permute-done.1 = f32[512,1024]{1,0:T(8,128)} collective-permute-done((f32[512,1024]{1,0:T(8,128)}, f32[512,1024]{1,0:T(8,128)}, u32[]{:S(2)}, u32[]{:S(2)}) %collective-permute-start.1) | collective-permute-done | bytes 2097184 | tf_op jit(solution)/shard_map/ppermute | solution.py:388
  505.7 6.5 %fusion.5 = (bf16[512,1024]{1,0:T(8,128)(2,1)S(1)}, bf16[512,1024]{1,0:T(8,128)(2,1)S(1)}) fusion(f32[1024,1024]{1,0:T(8,128)} %convert_element_type.18, f32[512,1024]{1,0:T(8,128)} %slice_add_fusion.5, f32[512,1024]{1,0:T(8,128)} %collective-permute-done, f32[1024]{0:T(1024)S(1)} %copy-done.37, f32[512,1024]{1,0:T(8,128)} %slice_add_fusion.4, ...), kind=kLoop, calls=%fused_computation.18 | loop fusion | flops 4194304 | bytes 14684160 | tf_op jit(solution)/shard_map/convert_element_type | solution.py:450
  519.1 12.3 %collective-permute-start.8 = (f32[8,1024]{1,0:T(8,128)S(1)}, f32[8,1024]{1,0:T(8,128)S(1)}, u32[]{:S(2)}, u32[]{:S(2)}) collective-permute-start(f32[8,1024]{1,0:T(8,128)S(1)} %add.427), channel_id=1, source_target_pairs={{0,2},{2,0},{1,3},{3,1},{4,6},{6,4},{5,7},{7,5},{8,10},{10,8},{9,1... | collective-permute-start | bytes 98312 | tf_op jit(solution)/shard_map/ppermute | solution.py:388
  546.2 5.3 fusion.9
  555.0 8.0 %copy.53 = f32[1024,2048]{1,0:T(8,128)} copy(f32[1024,2048]{1,0:T(8,128)} %bitcast.106) | data formatting | bytes 16777216
  (267 shorter events, 180.6 us)
Async XLA Ops:
  7.2 547.8 %all-gather.5.cloned.1.call-start = ((), (), s32[]{:S(2)}) async-start(), calls=%async_computation | async-start | bytes 8650752 | tf_op jit(solution)/shard_map/all_gather | solution.py:433
  68.3 8.5 %collective-permute-start.31 = (f32[16,32,2048]{2,1,0:T(8,128)}, f32[16,32,2048]{2,1,0:T(8,128)}, u32[]{:S(2)}, u32[]{:S(2)}) collective-permute-start(f32[16,32,2048]{2,1,0:T(8,128)} %constant_dynamic-slice_fusion.9), channel_id=1, source_target_pairs={{0,2},{2,0},{1,3},{3,1},{4,6},{6,4},{5,7},{7,5},{8,10},{10,8},{9,1... | collective-permute-start | bytes 12582920 | tf_op jit(solution)/shard_map/ppermute | solution.py:388
  83.1 27.6 %collective-permute-start.32 = (f32[8,32,2048]{2,1,0:T(8,128)S(1)}, f32[8,32,2048]{2,1,0:T(8,128)}, u32[]{:S(2)}, u32[]{:S(2)}) collective-permute-start(f32[8,32,2048]{2,1,0:T(8,128)S(1)} %constant_dynamic-slice_fusion.8), channel_id=1, source_target_pairs={{0,12},{2,50},{4,8},{6,54},{8,4},{10,58},{12,0},{14,62},{16,28},{1... | collective-permute-start | bytes 6291464 | tf_op jit(solution)/shard_map/ppermute | solution.py:373
  113.3 14.1 %collective-permute-start.33 = (f32[4,32,2048]{2,1,0:T(8,128)S(1)}, f32[4,32,2048]{2,1,0:T(8,128)}, u32[]{:S(2)}, u32[]{:S(2)}) collective-permute-start(f32[4,32,2048]{2,1,0:T(8,128)S(1)} %constant_dynamic-slice_fusion.7), channel_id=1, source_target_pairs={{0,48},{2,6},{4,52},{6,2},{8,56},{10,14},{12,60},{14,10},{16,32},{... | collective-permute-start | bytes 3145736 | tf_op jit(solution)/shard_map/ppermute | solution.py:373
  150.1 404.9 %all-gather.7.cloned.1.call-start = ((), (), s32[]{:S(2)}) async-start(), calls=%async_computation.1 | async-start | bytes 8650752 | tf_op jit(solution)/shard_map/all_gather | solution.py:432
  154.9 12.3 %collective-permute-start.37 = (f32[16,64,1024]{2,1,0:T(8,128)}, f32[16,64,1024]{2,1,0:T(8,128)}, u32[]{:S(2)}, u32[]{:S(2)}) collective-permute-start(f32[16,64,1024]{2,1,0:T(8,128)} %constant_dynamic-slice_fusion.4), channel_id=1, source_target_pairs={{0,2},{2,0},{1,3},{3,1},{4,6},{6,4},{5,7},{7,5},{8,10},{10,8},{9,1... | collective-permute-start | bytes 12582920 | tf_op jit(solution)/shard_map/ppermute | solution.py:388
  174.3 46.3 %collective-permute-start.38 = (f32[8,64,1024]{2,1,0:T(8,128)}, f32[8,64,1024]{2,1,0:T(8,128)}, u32[]{:S(2)}, u32[]{:S(2)}) collective-permute-start(f32[8,64,1024]{2,1,0:T(8,128)} %constant_dynamic-slice_fusion.3), channel_id=1, source_target_pairs={{0,4},{2,18},{4,0},{6,22},{8,12},{10,26},{12,8},{14,30},{16,20},{1... | collective-permute-start | bytes 6291464 | tf_op jit(solution)/shard_map/ppermute | solution.py:373
  218.5 59.5 %collective-permute-start.11 = (f32[2,1024,512]{2,1,0:T(8,128)}, f32[2,1024,512]{2,1,0:T(8,128)}, u32[]{:S(2)}, u32[]{:S(2)}) collective-permute-start(f32[2,1024,512]{2,1,0:T(8,128)} %constant_dynamic-slice_fusion.16), channel_id=1, source_target_pairs={{0,2},{2,0},{1,3},{3,1},{4,6},{6,4},{5,7},{7,5},{8,10},{10,8},{9,1... | collective-permute-start | bytes 12582920 | tf_op jit(solution)/shard_map/ppermute | solution.py:388
  225.6 15.2 %collective-permute-start.39 = (f32[4,64,1024]{2,1,0:T(8,128)}, f32[4,64,1024]{2,1,0:T(8,128)}, u32[]{:S(2)}, u32[]{:S(2)}) collective-permute-start(f32[4,64,1024]{2,1,0:T(8,128)} %constant_dynamic-slice_fusion.2), channel_id=1, source_target_pairs={{0,16},{2,14},{4,20},{6,10},{8,24},{10,6},{12,28},{14,2},{16,0},{1... | collective-permute-start | bytes 3145736 | tf_op jit(solution)/shard_map/ppermute | solution.py:373
  244.2 10.1 %collective-permute-start.40 = (f32[2,64,1024]{2,1,0:T(8,128)}, f32[2,64,1024]{2,1,0:T(8,128)}, u32[]{:S(2)}, u32[]{:S(2)}) collective-permute-start(f32[2,64,1024]{2,1,0:T(8,128)} %constant_dynamic-slice_fusion.1), channel_id=1, source_target_pairs={{0,12},{2,50},{4,8},{6,54},{8,4},{10,58},{12,0},{14,62},{16,28},{1... | collective-permute-start | bytes 1572872 | tf_op jit(solution)/shard_map/ppermute | solution.py:373
  256.5 14.4 %collective-permute-start.41 = (f32[1,64,1024]{2,1,0:T(8,128)S(1)}, f32[1,64,1024]{2,1,0:T(8,128)}, u32[]{:S(2)}, u32[]{:S(2)}) collective-permute-start(f32[1,64,1024]{2,1,0:T(8,128)S(1)} %constant_dynamic-slice_fusion), channel_id=1, source_target_pairs={{0,48},{2,6},{4,52},{6,2},{8,56},{10,14},{12,60},{14,10},{16,32},{... | collective-permute-start | bytes 786440 | tf_op jit(solution)/shard_map/ppermute | solution.py:373
  286.7 18.9 %collective-permute-start.21 = (f32[512,512]{1,0:T(8,128)}, f32[512,512]{1,0:T(8,128)}, u32[]{:S(2)}, u32[]{:S(2)}) collective-permute-start(f32[512,512]{1,0:T(8,128)} %dynamic-slice_bitcast_fusion), channel_id=1, source_target_pairs={{0,12},{2,50},{4,8},{6,54},{8,4},{10,58},{12,0},{14,62},{16,28},{1... | collective-permute-start | bytes 3145736 | tf_op jit(solution)/shard_map/ppermute | solution.py:373
  291.6 18.5 %collective-permute-start.12 = (f32[512,512]{1,0:T(8,128)}, f32[512,512]{1,0:T(8,128)}, u32[]{:S(2)}, u32[]{:S(2)}) collective-permute-start(f32[512,512]{1,0:T(8,128)} %dynamic-slice_bitcast_fusion.1), channel_id=1, source_target_pairs={{0,4},{2,18},{4,0},{6,22},{8,12},{10,26},{12,8},{14,30},{16,20},{1... | collective-permute-start | bytes 3145736 | tf_op jit(solution)/shard_map/ppermute | solution.py:373
  308.3 15.0 %collective-permute-start.22 = (f32[256,512]{1,0:T(8,128)}, f32[256,512]{1,0:T(8,128)}, u32[]{:S(2)}, u32[]{:S(2)}) collective-permute-start(f32[256,512]{1,0:T(8,128)} %constant_dynamic-slice_fusion.12), channel_id=1, source_target_pairs={{0,48},{2,6},{4,52},{6,2},{8,56},{10,14},{12,60},{14,10},{16,32},{... | collective-permute-start | bytes 1572872 | tf_op jit(solution)/shard_map/ppermute | solution.py:373
  312.4 19.7 %collective-permute-start.13 = (f32[256,512]{1,0:T(8,128)}, f32[256,512]{1,0:T(8,128)}, u32[]{:S(2)}, u32[]{:S(2)}) collective-permute-start(f32[256,512]{1,0:T(8,128)} %constant_dynamic-slice_fusion.15), channel_id=1, source_target_pairs={{0,16},{2,14},{4,20},{6,10},{8,24},{10,6},{12,28},{14,2},{16,0},{1... | collective-permute-start | bytes 1572872 | tf_op jit(solution)/shard_map/ppermute | solution.py:373
  316.7 157.4 %collective-permute-start = (f32[512,1024]{1,0:T(8,128)}, f32[512,1024]{1,0:T(8,128)}, u32[]{:S(2)}, u32[]{:S(2)}) collective-permute-start(f32[512,1024]{1,0:T(8,128)} %slice_add_fusion.5), channel_id=1, source_target_pairs={{0,1},{1,0},{2,3},{3,2},{4,5},{5,4},{6,7},{7,6},{8,9},{9,8},{10,11... | collective-permute-start | bytes 6291464 | tf_op jit(solution)/shard_map/ppermute | solution.py:388
  324.7 14.1 %collective-permute-start.23 = (f32[128,512]{1,0:T(8,128)S(1)}, f32[128,512]{1,0:T(8,128)S(1)}, u32[]{:S(2)}, u32[]{:S(2)}) collective-permute-start(f32[128,512]{1,0:T(8,128)S(1)} %constant_dynamic-slice_fusion.11), channel_id=1, source_target_pairs={{0,4},{2,18},{4,0},{6,22},{8,12},{10,26},{12,8},{14,30},{16,20},{1... | collective-permute-start | bytes 786440 | tf_op jit(solution)/shard_map/ppermute | solution.py:373
  333.3 10.3 %collective-permute-start.14 = (f32[128,512]{1,0:T(8,128)S(1)}, f32[128,512]{1,0:T(8,128)S(1)}, u32[]{:S(2)}, u32[]{:S(2)}) collective-permute-start(f32[128,512]{1,0:T(8,128)S(1)} %constant_dynamic-slice_fusion.14), channel_id=1, source_target_pairs={{0,12},{2,50},{4,8},{6,54},{8,4},{10,58},{12,0},{14,62},{16,28},{1... | collective-permute-start | bytes 786440 | tf_op jit(solution)/shard_map/ppermute | solution.py:373
  344.4 18.0 %collective-permute-start.25 = (f32[64,512]{1,0:T(8,128)S(1)}, f32[64,512]{1,0:T(8,128)S(1)}, u32[]{:S(2)}, u32[]{:S(2)}) collective-permute-start(f32[64,512]{1,0:T(8,128)S(1)} %dynamic-slice_add_fusion.15), channel_id=1, source_target_pairs={{0,64},{64,0},{1,65},{65,1},{2,66},{66,2},{3,67},{67,3},{4,68},{68... | collective-permute-start | bytes 393224 | tf_op jit(solution)/shard_map/ppermute | solution.py:388
  348.0 17.2 %collective-permute-start.16 = (f32[64,512]{1,0:T(8,128)S(1)}, f32[64,512]{1,0:T(8,128)S(1)}, u32[]{:S(2)}, u32[]{:S(2)}) collective-permute-start(f32[64,512]{1,0:T(8,128)S(1)} %dynamic-slice_add_fusion.16), channel_id=1, source_target_pairs={{0,64},{64,0},{1,65},{65,1},{2,66},{66,2},{3,67},{67,3},{4,68},{68... | collective-permute-start | bytes 393224 | tf_op jit(solution)/shard_map/ppermute | solution.py:388
  368.0 9.7 %collective-permute-start.27 = (f32[128,512]{1,0:T(8,128)S(1)}, f32[128,512]{1,0:T(8,128)S(1)}, u32[]{:S(2)}, u32[]{:S(2)}) collective-permute-start(f32[128,512]{1,0:T(8,128)S(1)} %maximum_select_fusion.10), channel_id=1, source_target_pairs={{0,4},{2,18},{4,0},{6,22},{8,12},{10,26},{12,8},{14,30},{16,20},{1... | collective-permute-start | bytes 786440 | tf_op jit(solution)/shard_map/ppermute | solution.py:379
  369.5 8.5 %collective-permute-start.18 = (f32[128,512]{1,0:T(8,128)S(1)}, f32[128,512]{1,0:T(8,128)S(1)}, u32[]{:S(2)}, u32[]{:S(2)}) collective-permute-start(f32[128,512]{1,0:T(8,128)S(1)} %maximum_select_fusion.9), channel_id=1, source_target_pairs={{0,12},{2,50},{4,8},{6,54},{8,4},{10,58},{12,0},{14,62},{16,28},{1... | collective-permute-start | bytes 786440 | tf_op jit(solution)/shard_map/ppermute | solution.py:379
  374.7 53.8 %collective-permute-start.2 = (f32[512,1024]{1,0:T(8,128)}, f32[512,1024]{1,0:T(8,128)}, u32[]{:S(2)}, u32[]{:S(2)}) collective-permute-start(f32[512,1024]{1,0:T(8,128)} %add_add_fusion.1), channel_id=1, source_target_pairs={{0,1},{1,0},{2,3},{3,2},{4,5},{5,4},{6,7},{7,6},{8,9},{9,8},{10,11... | collective-permute-start | bytes 6291464 | tf_op jit(solution)/shard_map/ppermute | solution.py:388
  377.7 11.3 %collective-permute-start.28 = (f32[256,512]{1,0:T(8,128)S(1)}, f32[256,512]{1,0:T(8,128)S(1)}, u32[]{:S(2)}, u32[]{:S(2)}) collective-permute-start(f32[256,512]{1,0:T(8,128)S(1)} %maximum_select_fusion.8), channel_id=1, source_target_pairs={{0,48},{2,6},{4,52},{6,2},{8,56},{10,14},{12,60},{14,10},{16,32},{... | collective-permute-start | bytes 1572872 | tf_op jit(solution)/shard_map/ppermute | solution.py:379
  378.0 12.5 %collective-permute-start.19 = (f32[256,512]{1,0:T(8,128)S(1)}, f32[256,512]{1,0:T(8,128)S(1)}, u32[]{:S(2)}, u32[]{:S(2)}) collective-permute-start(f32[256,512]{1,0:T(8,128)S(1)} %maximum_select_fusion.7), channel_id=1, source_target_pairs={{0,16},{2,14},{4,20},{6,10},{8,24},{10,6},{12,28},{14,2},{16,0},{1... | collective-permute-start | bytes 1572872 | tf_op jit(solution)/shard_map/ppermute | solution.py:379
  390.2 17.8 %collective-permute-start.29 = (f32[512,512]{1,0:T(8,128)}, f32[512,512]{1,0:T(8,128)}, u32[]{:S(2)}, u32[]{:S(2)}) collective-permute-start(f32[512,512]{1,0:T(8,128)} %maximum_select_fusion.6), channel_id=1, source_target_pairs={{0,12},{2,50},{4,8},{6,54},{8,4},{10,58},{12,0},{14,62},{16,28},{1... | collective-permute-start | bytes 3145736 | tf_op jit(solution)/shard_map/ppermute | solution.py:379
  391.6 20.8 %collective-permute-start.20 = (f32[512,512]{1,0:T(8,128)}, f32[512,512]{1,0:T(8,128)}, u32[]{:S(2)}, u32[]{:S(2)}) collective-permute-start(f32[512,512]{1,0:T(8,128)} %maximum_select_fusion.5), channel_id=1, source_target_pairs={{0,4},{2,18},{4,0},{6,22},{8,12},{10,26},{12,8},{14,30},{16,20},{1... | collective-permute-start | bytes 3145736 | tf_op jit(solution)/shard_map/ppermute | solution.py:379
  394.0 66.7 %collective-permute-start.3 = (f32[512,1024]{1,0:T(8,128)}, f32[512,1024]{1,0:T(8,128)}, u32[]{:S(2)}, u32[]{:S(2)}) collective-permute-start(f32[512,1024]{1,0:T(8,128)} %add_add_fusion), channel_id=1, source_target_pairs={{0,1},{1,0},{2,3},{3,2},{4,5},{5,4},{6,7},{7,6},{8,9},{9,8},{10,11... | collective-permute-start | bytes 6291464 | tf_op jit(solution)/shard_map/ppermute | solution.py:388
  408.0 97.7 %collective-permute-start.1 = (f32[512,1024]{1,0:T(8,128)}, f32[512,1024]{1,0:T(8,128)}, u32[]{:S(2)}, u32[]{:S(2)}) collective-permute-start(f32[512,1024]{1,0:T(8,128)} %slice_add_fusion.4), channel_id=1, source_target_pairs={{0,1},{1,0},{2,3},{3,2},{4,5},{5,4},{6,7},{7,6},{8,9},{9,8},{10,11... | collective-permute-start | bytes 6291464 | tf_op jit(solution)/shard_map/ppermute | solution.py:388
  417.5 123.3 %collective-permute-start.30 = (f32[2,1024,512]{2,1,0:T(8,128)}, f32[2,1024,512]{2,1,0:T(8,128)}, u32[]{:S(2)}, u32[]{:S(2)}) collective-permute-start(f32[2,1024,512]{2,1,0:T(8,128)} %pad_maximum_fusion.1), channel_id=1, source_target_pairs={{0,2},{2,0},{1,3},{3,1},{4,6},{6,4},{5,7},{7,5},{8,10},{10,8},{9,1... | collective-permute-start | bytes 12582920 | tf_op jit(solution)/shard_map/ppermute | solution.py:388
  471.4 40.8 %collective-permute-start.5 = (f32[8,1024]{1,0:T(8,128)S(1)}, f32[8,1024]{1,0:T(8,128)S(1)}, u32[]{:S(2)}, u32[]{:S(2)}) collective-permute-start(f32[8,1024]{1,0:T(8,128)S(1)} %add.424), channel_id=1, source_target_pairs={{0,16},{2,14},{4,20},{6,10},{8,24},{10,6},{12,28},{14,2},{16,0},{1... | collective-permute-start | bytes 98312 | tf_op jit(solution)/shard_map/ppermute | solution.py:393
  519.1 13.3 %collective-permute-start.8 = (f32[8,1024]{1,0:T(8,128)S(1)}, f32[8,1024]{1,0:T(8,128)S(1)}, u32[]{:S(2)}, u32[]{:S(2)}) collective-permute-start(f32[8,1024]{1,0:T(8,128)S(1)} %add.427), channel_id=1, source_target_pairs={{0,2},{2,0},{1,3},{3,1},{4,6},{6,4},{5,7},{7,5},{8,10},{10,8},{9,1... | collective-permute-start | bytes 98312 | tf_op jit(solution)/shard_map/ppermute | solution.py:388
  (55 other events, 537.6 us)
Sparse Core Ops, SparseCore 0:
  150.2 66.8 all-gather.4
  278.2 66.2 all-gather.6
